TPU v7x, 128 devices: a whole 4x4x4 slice. The times are simulated.
128 devices in a mesh: dp: 4 (over z_lo, core), axial: 32 (over x, y, z_hi).
Axes of the slice: x: 4, y: 4, z: 4 (z_hi: 2, z_lo: 2; z = z_hi * 2 + z_lo), core: 2. Of those that a mesh axis runs over, the one named last changes fastest.
Arguments:
- pair_act: bfloat16 [2560, 640, 128], P(('dp', 'axial')), parts along dimension 0, may hold values from -6 to 6
- ln_gain: float32 [128], replicated, may hold values from 0.25 to 1.75
- ln_shift: float32 [128], replicated, may hold values from -3 to 3
- w_qkv: bfloat16 [128, 384], replicated, as said below
- w_bias: bfloat16 [128, 4], replicated, as said below
- w_gate: bfloat16 [128, 128], replicated, may hold values from -0.5 to 0.5
- gate_shift: float32 [128], replicated, may hold values from -4 to 4
- w_out: bfloat16 [128, 128], replicated, may hold values from -0.5 to 0.5
- out_shift: float32 [128], replicated, may hold values from -3 to 3
Outputs:
- updated: bfloat16 [2560, 640, 128], P(('dp', 'axial')), parts along dimension 0
There are 4 independent parts, one for each index of `dp`. A program takes and returns all parts, laid end to end along the dimension named above; an argument that names none is the same for every part. Nothing has to cross between parts.
Inputs may be any that keep to these rules, and one draw needn't show every extreme that they name: `w_bias`: to one bias per head. `w_qkv`: keys and values.
All inputs are finite; a program needn't handle non-finite values.
Results may differ from a plain program's by a relative error of at most 0.0014.
The roundings to bfloat16 on the way count: a program that leaves them out, or rounds other values in their place, can miss the bound.
Values may be sent and summed in bfloat16 or wider, within the bound.
A program may use at most 128 MiB of HBM per device.

v0:
```python
import jax
import jax.numpy as jnp
from jax import lax
from jax.sharding import PartitionSpec as P

HEADS = 4
HDIM = 32


def normalize(pair_act, ln_gain, ln_shift):
    values = pair_act.astype(jnp.float32)
    center = jnp.mean(values, axis=-1, keepdims=True)
    spread = jnp.mean((values - center) ** 2, axis=-1, keepdims=True)
    return ((values - center) * lax.rsqrt(spread + 1e-05) * ln_gain + ln_shift).astype(jnp.bfloat16)


def project(normed, w_qkv):
    first, second, channels = normed.shape
    width = w_qkv.shape[1] // 3
    projected = jnp.dot(normed.reshape(-1, channels), w_qkv, preferred_element_type=jnp.float32)
    scaling = jnp.concatenate(
        [jnp.full((width,), HDIM ** (-0.5), jnp.float32), jnp.ones((2 * width,), jnp.float32)]
    )
    return (projected * scaling).astype(jnp.bfloat16).reshape(first, second, 3 * width)


def on_device(pair_act, ln_gain, ln_shift, w_qkv, w_bias, w_gate, gate_shift, w_out, out_shift):
    row_count, full_len, channels = pair_act.shape
    width = w_out.shape[0]
    normed = normalize(pair_act, ln_gain, ln_shift)
    bias_local = jnp.einsum(
        "kic,ch->hik", normed, w_bias, preferred_element_type=jnp.float32
    ).astype(jnp.bfloat16)
    projected = project(normed, w_qkv)
    qkv_cols = lax.all_to_all(projected, "axial", split_axis=1, concat_axis=0, tiled=True)
    bias_all = lax.all_gather(bias_local, "axial", axis=2, tiled=True)
    col_count = qkv_cols.shape[1]
    blocks = qkv_cols.reshape(full_len, col_count // 2, 2, 3, HEADS, HDIM)
    blocks = jnp.moveaxis(blocks, 1, 0)

    def column_pair(block):
        scores = jnp.einsum(
            "ijhd,kjhd->jhik", block[:, :, 0], block[:, :, 1], preferred_element_type=jnp.float32
        )
        scores = scores + bias_all[None].astype(jnp.float32)
        weights = jax.nn.softmax(scores, axis=-1).astype(jnp.bfloat16)
        result = jnp.einsum(
            "jhik,kjhd->ijhd", weights, block[:, :, 2], preferred_element_type=jnp.float32
        )
        return result.astype(jnp.bfloat16).reshape(full_len, 2, width)

    attended = lax.map(column_pair, blocks)
    attended = jnp.moveaxis(attended, 0, 1).reshape(full_len, col_count, width)
    attended_rows = lax.all_to_all(attended, "axial", split_axis=0, concat_axis=1, tiled=True)
    flat = normed.reshape(-1, channels)
    gate = jax.nn.sigmoid(jnp.dot(flat, w_gate, preferred_element_type=jnp.float32) + gate_shift)
    gated = (gate * attended_rows.reshape(-1, width).astype(jnp.float32)).astype(jnp.bfloat16)
    result = jnp.dot(gated, w_out, preferred_element_type=jnp.float32) + out_shift
    result = result + pair_act.reshape(-1, channels).astype(jnp.float32)
    return result.astype(jnp.bfloat16).reshape(row_count, full_len, channels)


def solution(mesh):
    in_specs = (P(("dp", "axial"), None, None), P(), P(), P(), P(), P(), P(), P(), P())
    out_specs = P(("dp", "axial"), None, None)
    return jax.shard_map(
        on_device, mesh=mesh, in_specs=in_specs, out_specs=out_specs, check_vma=False
    )
```

profile of v0, /device:TPU:0, one launch (start us, length us, event | category | flops | bytes accessed | tf_op | source)
XLA Modules:
  0.0 762.3 jit_solution(13176805961015883640)
XLA Ops:
  6.5 3.0 convert_reduce_fusion
  9.6 5.2 multiply_reduce_fusion
  14.8 4.4 add_convert_fusion
  19.3 2.9 multiply_convert_fusion
  22.2 34.5 %copy.38 = bf16[20,640,384]{2,0,1:T(8,128)(2,1)} copy(bf16[20,640,384]{2,1,0:T(8,128)(2,1)S(1)} %bitcast.68) | data formatting | bytes 19660800 | tf_op jit(solution)/shard_map/reshape | solution.py:24
  56.7 10.9 %all-to-all-start = ((bf16[20,640,384]{2,0,1:T(8,128)(2,1)}), bf16[20,640,384]{2,0,1:T(8,128)(2,1)}, u32[]{:S(2)}, u32[]{:S(2)}) async-start(bf16[20,640,384]{2,0,1:T(8,128)(2,1)} %copy.38), calls=%async_computation | async-start | bytes 23592960 | tf_op jit(solution)/shard_map/all_to_all | solution.py:35
  69.5 227.1 %all-gather.2.cloned.1.call-done = bf16[4,640,640]{1,0,2:T(4,128)(2,1)} async-done(((bf16[4,640,20]{1,0,2:T(4,128)(2,1)}), bf16[4,640,640]{1,0,2:T(4,128)(2,1)}) %all-gather.2.cloned.1.call-update) | async-done | bytes 3276816 | tf_op jit(solution)/shard_map/all_gather | solution.py:36
  299.0 11.1 %copy.40 = bf16[32,20,20,384]{3,2,1,0:T(8,128)(2,1)} copy(bf16[32,20,20,384]{3,1,2,0:T(8,128)(2,1)} %bitcast.10) | data formatting | bytes 19660800 | tf_op jit(solution)/shard_map/all_to_all | solution.py:35
  310.1 52.0 %reshape.52 = bf16[640,10,2,3,4,32]{5,4,3,2,1,0:T(4,128)(2,1)} reshape(bf16[32,20,20,384]{3,2,1,0:T(8,128)(2,1)} %copy.40) | data formatting | bytes 19660800 | tf_op jit(solution)/shard_map/reshape | solution.py:38
  362.1 45.9 %copy.41 = bf16[10,640,2,3,4,32]{1,5,4,2,3,0:T(8,128)(2,1)} copy(bf16[10,640,2,3,4,32]{5,4,3,2,0,1:T(4,128)(2,1)} %bitcast.67) | data formatting | bytes 19660800 | tf_op jit(solution)/shard_map/while | solution.py:52
  408.0 237.7 %while.10 = (s32[]{:T(128)}, bf16[10,640,2,128]{1,3,2,0:T(8,128)(2,1)}, bf16[10,640,2,3,4,32]{1,5,4,2,3,0:T(8,128)(2,1)}, bf16[4,640,640]{1,2,0:T(8,128)(2,1)S(1)}, s32[]{:T(128)}) while((s32[]{:T(128)}, bf16[10,640,2,128]{1,3,2,0:T(8,128)(2,1)}, bf16[10,640,2,3,4,32]{1,5,4,2,3,0:T(8,128)(2,1)}, bf16[4,640,640]{1,2,0:T(8,128)(2,1)S(1)}, ...), condition=%wide.region_5.6_spmd, body=%wide.region_2.5_spmd.sunk | while | flops 437617280 | bytes 46572096 | solution.py:52
  410.3 3.1 convert_element_type.96
  413.4 11.7 %fusion.30 = (f32[2,4,640]{2,1,0:T(4,128)S(1)}, f32[2,4,640,640]{2,3,1,0:T(8,128)}) fusion(f32[4,640,640]{1,2,0:T(8,128)} %convert_element_type.96, bf16[640,2,3,4,32]{0,4,3,1,2:T(8,128)(2,1)} %dynamic-slice_bitcast_fusion.2), kind=kOutput, calls=%fused_computation.36.clone.1 | convolution fusion | flops 219546240 | bytes 20336640 | tf_op jit(solution)/shard_map/while/body/eval_jaxpr/sub | solution.py:46
  425.0 6.0 fusion.31
  434.0 3.1 convert_element_type.96
  437.2 11.7 %fusion.30 = (f32[2,4,640]{2,1,0:T(4,128)S(1)}, f32[2,4,640,640]{2,3,1,0:T(8,128)}) fusion(f32[4,640,640]{1,2,0:T(8,128)} %convert_element_type.96, bf16[640,2,3,4,32]{0,4,3,1,2:T(8,128)(2,1)} %dynamic-slice_bitcast_fusion.2), kind=kOutput, calls=%fused_computation.36.clone.1 | convolution fusion | flops 219546240 | bytes 20336640 | tf_op jit(solution)/shard_map/while/body/eval_jaxpr/sub | solution.py:46
  448.8 6.0 fusion.31
  457.8 3.1 convert_element_type.96
  460.9 11.7 %fusion.30 = (f32[2,4,640]{2,1,0:T(4,128)S(1)}, f32[2,4,640,640]{2,3,1,0:T(8,128)}) fusion(f32[4,640,640]{1,2,0:T(8,128)} %convert_element_type.96, bf16[640,2,3,4,32]{0,4,3,1,2:T(8,128)(2,1)} %dynamic-slice_bitcast_fusion.2), kind=kOutput, calls=%fused_computation.36.clone.1 | convolution fusion | flops 219546240 | bytes 20336640 | tf_op jit(solution)/shard_map/while/body/eval_jaxpr/sub | solution.py:46
  472.6 6.0 fusion.31
  481.6 3.1 convert_element_type.96
  484.7 11.7 %fusion.30 = (f32[2,4,640]{2,1,0:T(4,128)S(1)}, f32[2,4,640,640]{2,3,1,0:T(8,128)}) fusion(f32[4,640,640]{1,2,0:T(8,128)} %convert_element_type.96, bf16[640,2,3,4,32]{0,4,3,1,2:T(8,128)(2,1)} %dynamic-slice_bitcast_fusion.2), kind=kOutput, calls=%fused_computation.36.clone.1 | convolution fusion | flops 219546240 | bytes 20336640 | tf_op jit(solution)/shard_map/while/body/eval_jaxpr/sub | solution.py:46
  496.4 6.0 fusion.31
  505.4 3.1 convert_element_type.96
  508.5 11.7 %fusion.30 = (f32[2,4,640]{2,1,0:T(4,128)S(1)}, f32[2,4,640,640]{2,3,1,0:T(8,128)}) fusion(f32[4,640,640]{1,2,0:T(8,128)} %convert_element_type.96, bf16[640,2,3,4,32]{0,4,3,1,2:T(8,128)(2,1)} %dynamic-slice_bitcast_fusion.2), kind=kOutput, calls=%fused_computation.36.clone.1 | convolution fusion | flops 219546240 | bytes 20336640 | tf_op jit(solution)/shard_map/while/body/eval_jaxpr/sub | solution.py:46
  520.1 6.0 fusion.31
  529.1 3.1 convert_element_type.96
  532.2 11.7 %fusion.30 = (f32[2,4,640]{2,1,0:T(4,128)S(1)}, f32[2,4,640,640]{2,3,1,0:T(8,128)}) fusion(f32[4,640,640]{1,2,0:T(8,128)} %convert_element_type.96, bf16[640,2,3,4,32]{0,4,3,1,2:T(8,128)(2,1)} %dynamic-slice_bitcast_fusion.2), kind=kOutput, calls=%fused_computation.36.clone.1 | convolution fusion | flops 219546240 | bytes 20336640 | tf_op jit(solution)/shard_map/while/body/eval_jaxpr/sub | solution.py:46
  543.9 6.0 fusion.31
  552.9 3.1 convert_element_type.96
  556.0 11.7 %fusion.30 = (f32[2,4,640]{2,1,0:T(4,128)S(1)}, f32[2,4,640,640]{2,3,1,0:T(8,128)}) fusion(f32[4,640,640]{1,2,0:T(8,128)} %convert_element_type.96, bf16[640,2,3,4,32]{0,4,3,1,2:T(8,128)(2,1)} %dynamic-slice_bitcast_fusion.2), kind=kOutput, calls=%fused_computation.36.clone.1 | convolution fusion | flops 219546240 | bytes 20336640 | tf_op jit(solution)/shard_map/while/body/eval_jaxpr/sub | solution.py:46
  567.7 6.0 fusion.31
  576.7 3.1 convert_element_type.96
  579.8 11.7 %fusion.30 = (f32[2,4,640]{2,1,0:T(4,128)S(1)}, f32[2,4,640,640]{2,3,1,0:T(8,128)}) fusion(f32[4,640,640]{1,2,0:T(8,128)} %convert_element_type.96, bf16[640,2,3,4,32]{0,4,3,1,2:T(8,128)(2,1)} %dynamic-slice_bitcast_fusion.2), kind=kOutput, calls=%fused_computation.36.clone.1 | convolution fusion | flops 219546240 | bytes 20336640 | tf_op jit(solution)/shard_map/while/body/eval_jaxpr/sub | solution.py:46
  591.4 6.0 fusion.31
  600.5 3.1 convert_element_type.96
  603.6 11.7 %fusion.30 = (f32[2,4,640]{2,1,0:T(4,128)S(1)}, f32[2,4,640,640]{2,3,1,0:T(8,128)}) fusion(f32[4,640,640]{1,2,0:T(8,128)} %convert_element_type.96, bf16[640,2,3,4,32]{0,4,3,1,2:T(8,128)(2,1)} %dynamic-slice_bitcast_fusion.2), kind=kOutput, calls=%fused_computation.36.clone.1 | convolution fusion | flops 219546240 | bytes 20336640 | tf_op jit(solution)/shard_map/while/body/eval_jaxpr/sub | solution.py:46
  615.2 6.0 fusion.31
  624.2 3.1 convert_element_type.96
  627.3 11.7 %fusion.30 = (f32[2,4,640]{2,1,0:T(4,128)S(1)}, f32[2,4,640,640]{2,3,1,0:T(8,128)}) fusion(f32[4,640,640]{1,2,0:T(8,128)} %convert_element_type.96, bf16[640,2,3,4,32]{0,4,3,1,2:T(8,128)(2,1)} %dynamic-slice_bitcast_fusion.2), kind=kOutput, calls=%fused_computation.36.clone.1 | convolution fusion | flops 219546240 | bytes 20336640 | tf_op jit(solution)/shard_map/while/body/eval_jaxpr/sub | solution.py:46
  639.0 6.0 fusion.31
  645.7 6.3 copy.44
  652.0 66.2 %all_to_all.24 = bf16[640,20,128]{2,1,0:T(8,128)(2,1)S(1)} all-to-all(bf16[640,20,128]{2,1,0:T(8,128)(2,1)} %copy.44), channel_id=1, replica_groups=mesh['dp'=4,'axial'=32] {'axial'}, dimensions={0} | all-to-all | bytes 6553600 | tf_op jit(solution)/shard_map/all_to_all | solution.py:54
  718.2 3.5 copy_convert_fusion
  721.7 8.2 %reshape.57 = f32[32,20,20,128]{3,1,0,2:T(8,128)} reshape(f32[640,20,128]{2,0,1:T(8,128)} %copy_convert_fusion) | data formatting | bytes 13107200 | tf_op jit(solution)/shard_map/convert_element_type | solution.py:57
  729.9 10.3 %copy.46 = f32[20,32,20,128]{3,2,1,0:T(8,128)} copy(f32[20,32,20,128]{3,0,1,2:T(8,128)} %bitcast.71) | data formatting | bytes 13107200 | tf_op jit(solution)/shard_map/convert_element_type | solution.py:57
  740.2 8.8 %reshape.55 = f32[12800,128]{1,0:T(8,128)} reshape(f32[20,32,20,128]{3,2,1,0:T(8,128)} %copy.46) | data formatting | bytes 13107200 | tf_op jit(solution)/shard_map/convert_element_type | solution.py:57
  749.0 6.4 fusion.14
  (54 shorter events, 34.6 us)
Async XLA Ops:
  6.5 12.7 %copy-start = (bf16[128,384]{1,0:T(8,128)(2,1)S(1)}, bf16[128,384]{1,0:T(8,128)(2,1)}, u32[]{:S(2)}) copy-start(bf16[128,384]{1,0:T(8,128)(2,1)} %param.14) | copy-start | bytes 294916
  6.5 12.7 %copy-start.5 = (f32[384]{0:T(512)S(1)}, f32[384]{0:T(512)}, u32[]{:S(2)}) copy-start(f32[384]{0:T(512)} %constant.30.clone.1) | copy-start | bytes 4612
  6.5 8.3 %copy-start.4 = (bf16[20,640,128]{2,1,0:T(8,128)(2,1)S(1)}, bf16[20,640,128]{2,1,0:T(8,128)(2,1)}, u32[]{:S(2)}) copy-start(bf16[20,640,128]{2,1,0:T(8,128)(2,1)} %param.11) | copy-start | bytes 9830404
  6.5 8.3 %copy-start.8 = (f32[128]{0:T(128)S(1)}, f32[128]{0:T(128)}, u32[]{:S(2)}) copy-start(f32[128]{0:T(128)} %param.12) | copy-start | bytes 1540
  6.5 8.3 %copy-start.7 = (f32[128]{0:T(128)S(1)}, f32[128]{0:T(128)}, u32[]{:S(2)}) copy-start(f32[128]{0:T(128)} %param.13) | copy-start | bytes 1540
  19.2 48.6 %copy-start.2 = (bf16[20,640,128]{2,1,0:T(8,128)(2,1)}, bf16[20,640,128]{2,1,0:T(8,128)(2,1)S(1)}, u32[]{:S(2)}) copy-start(bf16[20,640,128]{2,1,0:T(8,128)(2,1)S(1)} %add_convert_fusion) | copy-start | bytes 9830404
  56.7 11.2 %copy-start.6 = (bf16[128,4]{0,1:T(4,128)(2,1)S(1)}, bf16[128,4]{0,1:T(4,128)(2,1)}, u32[]{:S(2)}) copy-start(bf16[128,4]{0,1:T(4,128)(2,1)} %param.15) | copy-start | bytes 3076
  56.7 242.3 %all-to-all-start = ((bf16[20,640,384]{2,0,1:T(8,128)(2,1)}), bf16[20,640,384]{2,0,1:T(8,128)(2,1)}, u32[]{:S(2)}, u32[]{:S(2)}) async-start(bf16[20,640,384]{2,0,1:T(8,128)(2,1)} %copy.38), calls=%async_computation | async-start | bytes 23592960 | tf_op jit(solution)/shard_map/all_to_all | solution.py:35
  67.6 229.0 %all-gather.2.cloned.1.call-start = ((), (), s32[]{:S(2)}) async-start(), calls=%async_computation.2 | async-start | bytes 3379200 | tf_op jit(solution)/shard_map/all_gather | solution.py:36
  740.1 8.8 %copy-start.3 = (bf16[20,640,128]{2,1,0:T(8,128)(2,1)S(1)}, bf16[20,640,128]{2,1,0:T(8,128)(2,1)}, u32[]{:S(2)}) copy-start(bf16[20,640,128]{2,1,0:T(8,128)(2,1)} %copy-done.2) | copy-start | bytes 9830404
  740.1 8.8 %copy-start.9 = (bf16[128,128]{1,0:T(8,128)(2,1)S(1)}, bf16[128,128]{1,0:T(8,128)(2,1)}, u32[]{:S(2)}) copy-start(bf16[128,128]{1,0:T(8,128)(2,1)} %param.18) | copy-start | bytes 98308
  740.1 8.8 %copy-start.10 = (bf16[128,128]{1,0:T(8,128)(2,1)S(1)}, bf16[128,128]{1,0:T(8,128)(2,1)}, u32[]{:S(2)}) copy-start(bf16[128,128]{1,0:T(8,128)(2,1)} %param.16) | copy-start | bytes 98308
  740.1 8.8 %copy-start.11 = (f32[128]{0:T(128)S(1)}, f32[128]{0:T(128)}, u32[]{:S(2)}) copy-start(f32[128]{0:T(128)} %param.19) | copy-start | bytes 1540
  740.2 8.9 %copy-start.12 = (f32[128]{0:T(128)S(1)}, f32[128]{0:T(128)}, u32[]{:S(2)}) copy-start(f32[128]{0:T(128)} %param.17) | copy-start | bytes 1540
  749.0 6.4 copy-start.1
Sparse Core Ops, SparseCore 0:
  71.4 225.1 all-gather.1
where the time goes:
time: 766 us; the launch traced here: 762 us
  waiting for transfers between devices  227 us (30%)
  local copies, waits for them, and re-layouts  210 us (27%)
  matrix products  187 us (24%)
  blocking collectives  66.2 us (9%)
  other arithmetic  47.2 us (6%)
  between operations  13.6 us (2%)
  starting transfers between devices  11.2 us (1%)
    all_gather x1, waiting for transfers between devices, on_device(): bias_all = lax.all_gather(bias_local, 'axial', axis=2, tiled=True)  227 us
    sub x10, matrix products, column_pair(): weights = jax.nn.softmax(scores, axis=-1).astype(jnp.bfloat16)  117 us
    all_to_all x1, blocking collectives, on_device(): lax.all_to_all(attended, 'axial', split_axis=0, concat_axis=1, tiled=True)  66.2 us
    dot_general x10, matrix products, column_pair(): jnp.einsum('jhik,kjhd->ijhd', weights, block[:, :, 2], preferred_element_...  59.7 us
    reshape x1, local copies, waits for them, and re-layouts, on_device(): blocks = qkv_cols.reshape(full_len, col_count // 2, 2, 3, HEADS, HDIM)  52 us
    while x2, local copies, waits for them, and re-layouts, on_device(): attended = lax.map(column_pair, blocks)  48.3 us
    reshape x1, local copies, waits for them, and re-layouts, project(): (projected * scaling).astype(jnp.bfloat16).reshape(first, second, 3 * width)  34.5 us
    convert_element_type x10, other arithmetic, column_pair(): scores = scores + bias_all[None].astype(jnp.float32)  31.1 us
  transfers between devices with their start and end apart: 2, of which 1 were waited for; matrix products, arithmetic and copies ran while one was open for 1% of the time, Pallas kernels for 0%

commit v1 on v0

v1 whole, which is shorter than its diff:
```python
import functools

import jax
import jax.numpy as jnp
from jax import lax
from jax.experimental import pallas as pl
from jax.experimental.pallas import tpu as pltpu
from jax.sharding import PartitionSpec as P

HEADS = 4
HDIM = 32
CH = 128
MESH = pl.DeviceIdType.MESH
F32 = jnp.float32
BF16 = jnp.bfloat16
NT = (((1,), (1,)), ((), ()))


def normalize(values, gain, shift):
    center = jnp.mean(values, axis=-1, keepdims=True)
    spread = jnp.mean((values - center) ** 2, axis=-1, keepdims=True)
    return (values - center) * lax.rsqrt(spread + 1e-05) * gain + shift


def upper_half(shape):
    return lax.broadcasted_iota(jnp.int32, shape, len(shape) - 2) < 4


def balanced_offsets():
    rest = [(x, y, z) for x in range(4) for y in range(4) for z in range(2) if x or y or z]

    def load(o):
        out = [0] * 6
        for axis, step in enumerate((o[0], o[1], 2 * o[2])):
            out[2 * axis] += step in (1, 2)
            out[2 * axis + 1] += step in (2, 3)
        return out

    total, order = [0] * 6, []
    while rest:
        def cost(o):
            new = [t + a for t, a in zip(total, load(o))]
            return max(new) * 100 + sum(n * n for n in new), -sum(load(o))
        best = min(rest, key=cost)
        rest.remove(best)
        order.append(best)
        total = [t + a for t, a in zip(total, load(best))]
    return order


OFFSETS = balanced_offsets()


def kernel(
    n, pair, gain, shift, wq_t, wk, wv_t, wbias_t, wgate, gate_shift, wout, out_shift, out,
    send_in, recv_in, send_out, recv_out, bias_send, bias_recv, bias_all,
    mix, normed, update, rows_bias, q_t, keys, v_t, att_t,
    ss_bias, rs_bias, ss_in, rs_in, ss_out, rs_out, local_sem,
):
    rows, full, _ = pair.shape
    groups = send_in.shape[0]
    block = 4 * rows
    wide = n * 4
    me = lax.axis_index("axial")
    x, y, z = me // 8, lax.rem(me // 2, 4), lax.rem(me, 2)

    def peer(o):
        return (lax.rem(x + o[0], 4) * 4 + lax.rem(y + o[1], 4)) * 2 + lax.rem(z + o[2], 2)

    def bias_row(k, _):
        normal = normalize(pair[k].astype(F32), gain[...], shift[...]).astype(BF16)
        line = lax.dot_general(wbias_t[...], normal, NT, preferred_element_type=F32)
        for h in range(HEADS):
            place = jnp.where(k < 16, h * 16 + k, 4 * h + 48 + k)
            rows_bias[pl.ds(place, 1), :] = line[h : h + 1, :]
        return 0

    lax.fori_loop(0, rows, bias_row, 0)
    bias_send[...] = rows_bias[...].astype(BF16)

    def assemble(g, _):
        top = upper_half((n // 2, 8, CH))
        for a in range(0, rows, 2):
            even = pair[a, pl.ds(pl.multiple_of(g * wide, wide), wide), :].astype(F32).reshape(n // 2, 8, CH)
            odd = pair[a + 1, pl.ds(pl.multiple_of(g * wide, wide), wide), :].astype(F32).reshape(n // 2, 8, CH)
            mix[:, 0, 4 * a : 4 * a + 8, :] = jnp.where(top, even, pltpu.roll(odd, 4, 1))
            mix[:, 1, 4 * a : 4 * a + 8, :] = jnp.where(top, pltpu.roll(even, 4, 1), odd)
        send_in[g] = mix[...].astype(BF16).reshape(n, block, CH)
        return 0

    lax.fori_loop(0, groups, assemble, 0)

    barrier = pltpu.get_barrier_semaphore()
    for o in OFFSETS:
        pl.semaphore_signal(barrier, inc=1, device_id={"axial": peer(o)}, device_id_type=MESH)
    pl.semaphore_wait(barrier, n - 1)

    def remote(src, dst, ss, rs, to):
        return pltpu.make_async_remote_copy(
            src_ref=src, dst_ref=dst, send_sem=ss, recv_sem=rs, device_id={"axial": to}, device_id_type=MESH
        )

    def wait_bytes(ref, sem):
        pltpu.make_async_copy(ref, ref, sem).wait()

    for o in OFFSETS:
        remote(bias_send, bias_recv.at[me], ss_bias, rs_bias, peer(o)).start()
    own_bias = pltpu.make_async_copy(bias_send, bias_recv.at[me], local_sem.at[0])
    own_bias.start()

    def send_group(g, _):
        for o in OFFSETS:
            to = peer(o)
            remote(send_in.at[g, to], recv_in.at[g, me], ss_in.at[g], rs_in.at[g], to).start()
        pltpu.make_async_copy(send_in.at[g, me], recv_in.at[g, me], rs_in.at[g]).start()
        return 0

    lax.fori_loop(0, groups, send_group, 0)

    own_bias.wait()
    wait_bytes(bias_recv.at[pl.ds(0, n - 1)], rs_bias)

    def spread_bias(p, _):
        top = upper_half((8, full))
        turn = lambda tile: pltpu.roll(tile, 4, 0)
        first = bias_recv[2 * p].astype(F32)
        second = bias_recv[2 * p + 1].astype(F32)
        for h in range(HEADS):
            tail = slice(64 + h // 2 * 8, 72 + h // 2 * 8)
            first_tail, second_tail = first[tail], second[tail]
            if h % 2:
                first_tail = turn(first_tail)
            else:
                second_tail = turn(second_tail)
            low, high = turn(second[16 * h : 16 * h + 8]), turn(second[16 * h + 8 : 16 * h + 16])
            start = pl.multiple_of(2 * rows * p, 8)
            bias_all[h, pl.ds(start, 16), :] = first[16 * h : 16 * h + 16]
            bias_all[h, pl.ds(pl.multiple_of(start + 16, 8), 8), :] = jnp.where(top, first_tail, low)
            bias_all[h, pl.ds(pl.multiple_of(start + 24, 8), 8), :] = jnp.where(top, low, high)
            bias_all[h, pl.ds(pl.multiple_of(start + 32, 8), 8), :] = jnp.where(top, high, second_tail)
        return 0

    lax.fori_loop(0, n // 2, spread_bias, 0)

    def group(g, _):
        wait_bytes(recv_in.at[g], rs_in.at[g])

        def norm_block(s, _):
            values = recv_in[g, pl.ds(4 * s, 4)].astype(F32).reshape(4 * block, CH)
            normed[pl.ds(pl.multiple_of(4 * block * s, 4 * block), 4 * block), :] = normalize(
                values, gain[...], shift[...]
            )
            return 0

        lax.fori_loop(0, n // 4, norm_block, 0)

        def column(b, _):
            normal = normed[pl.ds(b, full, stride=4), :].astype(BF16)
            queries = lax.dot_general(wq_t[...], normal, NT, preferred_element_type=F32)
            q_t[...] = (queries * HDIM ** (-0.5)).astype(BF16)
            keys[...] = jnp.dot(normal, wk[...], preferred_element_type=F32).astype(BF16)
            v_t[...] = lax.dot_general(wv_t[...], normal, NT, preferred_element_type=F32).astype(BF16)
            gate = jax.nn.sigmoid(jnp.dot(normal, wgate[...], preferred_element_type=F32) + gate_shift[...])

            def head(h, _):
                mine = lax.broadcasted_iota(jnp.int32, (CH, full), 0) // HDIM == h
                query = jnp.where(mine, q_t[...], jnp.zeros((), BF16))
                scores = jnp.dot(keys[...], query, preferred_element_type=F32) + bias_all[h]
                top = jnp.max(scores, axis=0, keepdims=True)
                raised = jnp.exp(scores - top)
                weights = (raised * (1.0 / jnp.sum(raised, axis=0, keepdims=True))).astype(BF16)
                own = pl.ds(pl.multiple_of(h * HDIM, HDIM), HDIM)
                att_t[own, :] = jnp.dot(v_t[own, :], weights, preferred_element_type=F32)
                return 0

            lax.fori_loop(0, HEADS, head, 0)
            attended = att_t[...].T.astype(BF16).astype(F32)
            gated = (gate * attended).astype(BF16)
            update[pl.ds(b, full, stride=4), :] = (
                jnp.dot(gated, wout[...], preferred_element_type=F32) + out_shift[...]
            )
            return 0

        lax.fori_loop(0, 4, column, 0)

        def finish(s, _):
            values = recv_in[g, pl.ds(4 * s, 4)].astype(F32)
            total = update[pl.ds(pl.multiple_of(4 * block * s, 4 * block), 4 * block), :].reshape(4, block, CH) + values
            send_out[g, pl.ds(4 * s, 4)] = total.astype(BF16)
            return 0

        lax.fori_loop(0, n // 4, finish, 0)
        for o in OFFSETS:
            to = peer(o)
            remote(send_out.at[g, to], recv_out.at[g, me], ss_out.at[g], rs_out.at[g], to).start()
        pltpu.make_async_copy(send_out.at[g, me], recv_out.at[g, me], rs_out.at[g]).start()
        return 0

    lax.fori_loop(0, groups, group, 0)

    def collect(g, _):
        wait_bytes(recv_out.at[g], rs_out.at[g])
        top = upper_half((n // 2, 8, CH))
        mix[...] = recv_out[g].astype(F32).reshape(n // 2, 2, block, CH)
        for a in range(0, rows, 2):
            first = mix[:, 0, 4 * a : 4 * a + 8, :]
            second = mix[:, 1, 4 * a : 4 * a + 8, :]
            even = jnp.where(top, first, pltpu.roll(second, 4, 1))
            odd = jnp.where(top, pltpu.roll(first, 4, 1), second)
            here = pl.ds(pl.multiple_of(g * wide, wide), wide)
            out[a, here, :] = even.reshape(wide, CH).astype(BF16)
            out[a + 1, here, :] = odd.reshape(wide, CH).astype(BF16)
        return 0

    lax.fori_loop(0, groups, collect, 0)

    wait_bytes(bias_recv.at[pl.ds(0, n - 1)], ss_bias)

    def drain(g, _):
        wait_bytes(send_in.at[g, pl.ds(0, n - 1)], ss_in.at[g])
        wait_bytes(send_out.at[g, pl.ds(0, n - 1)], ss_out.at[g])
        return 0

    lax.fori_loop(0, groups, drain, 0)


def on_device(n, pair_act, ln_gain, ln_shift, w_qkv, w_bias, w_gate, gate_shift, w_out, out_shift):
    rows, full, channels = pair_act.shape
    groups = full // (4 * n)
    block = 4 * rows
    wbias_t = jnp.concatenate([w_bias.T, jnp.zeros((16 - HEADS, channels), BF16)], axis=0)
    vmem = pl.BlockSpec(memory_space=pltpu.VMEM)
    dma = pltpu.SemaphoreType.DMA
    return pl.pallas_call(
        functools.partial(kernel, n),
        out_shape=jax.ShapeDtypeStruct(pair_act.shape, BF16),
        in_specs=[vmem] * 11,
        out_specs=vmem,
        scratch_shapes=[
            pltpu.VMEM((groups, n, block, CH), BF16),
            pltpu.VMEM((groups, n, block, CH), BF16),
            pltpu.VMEM((groups, n, block, CH), BF16),
            pltpu.VMEM((groups, n, block, CH), BF16),
            pltpu.VMEM((HEADS * rows, full), BF16),
            pltpu.VMEM((n, HEADS * rows, full), BF16),
            pltpu.VMEM((HEADS, full, full), F32),
            pltpu.VMEM((n // 2, 2, block, CH), F32),
            pltpu.VMEM((n * block, CH), F32),
            pltpu.VMEM((n * block, CH), F32),
            pltpu.VMEM((HEADS * rows, full), F32),
            pltpu.VMEM((CH, full), BF16),
            pltpu.VMEM((full, CH), BF16),
            pltpu.VMEM((CH, full), BF16),
            pltpu.VMEM((CH, full), F32),
            dma, dma, dma((groups,)), dma((groups,)), dma((groups,)), dma((groups,)), dma((1,)),
        ],
        compiler_params=pltpu.CompilerParams(
            collective_id=0, has_side_effects=True, vmem_limit_bytes=58 * 2**20
        ),
        name="triangle",
    )(
        pair_act, ln_gain[None], ln_shift[None], w_qkv[:, :CH].T, w_qkv[:, CH : 2 * CH], w_qkv[:, 2 * CH :].T,
        wbias_t, w_gate, gate_shift[None], w_out, out_shift[None],
    )


def solution(mesh):
    in_specs = (P(("dp", "axial"), None, None), P(), P(), P(), P(), P(), P(), P(), P())
    out_specs = P(("dp", "axial"), None, None)
    return jax.shard_map(
        functools.partial(on_device, mesh.shape["axial"]),
        mesh=mesh, in_specs=in_specs, out_specs=out_specs, check_vma=False,
    )
```

time: 766 us -> 195 us (0.25)
  waiting for transfers between devices: 227 us -> 0 us
  local copies, waits for them, and re-layouts: 210 us -> 8.08 us
  matrix products: 187 us -> 0 us
  Pallas kernels: 0 us -> 186 us
  blocking collectives: 66.2 us -> 0 us
  other arithmetic: 47.2 us -> 0 us
  between operations: 13.6 us -> 0.01 us
  starting transfers between devices: 11.2 us -> 0 us
    all_gather x1 -> x0, waiting for transfers between devices: 227 us -> none  [on_device(): bias_all = lax.all_gather(bias_local, 'axial', axis=2, tiled=True)]
    pallas_call x0 -> x1, Pallas kernels: none -> 186 us  [on_device(): pl.pallas_call(functools.partial(kernel, n), out_shape=jax.ShapeDtypeStru...]
    sub x10 -> x0, matrix products: 117 us -> none  [column_pair(): weights = jax.nn.softmax(scores, axis=-1).astype(jnp.bfloat16)]
    reshape x3 -> x0, local copies, waits for them, and re-layouts: 92.8 us -> none  [the longest x1 52 us: on_device(): blocks = qkv_cols.reshape(full_len, col_count // 2, 2, 3, HEADS, HDIM)]
    dot_general x13 -> x0, matrix products: 70.6 us -> none  [the longest x10 59.7 us: column_pair(): jnp.einsum('jhik,kjhd->ijhd', weights, block[:, :, 2], preferred_element_...]
    all_to_all x1 -> x0, blocking collectives: 66.2 us -> none  [on_device(): lax.all_to_all(attended, 'axial', split_axis=0, concat_axis=1, tiled=True)]
    while x2 -> x0, local copies, waits for them, and re-layouts: 48.3 us -> none  [on_device(): attended = lax.map(column_pair, blocks)]
    convert_element_type x12 -> x0, other arithmetic: 38.9 us -> none  [the longest x10 31.1 us: column_pair(): scores = scores + bias_all[None].astype(jnp.float32)]
  transfers between devices with their start and end apart: 2 -> 0, of which waited for: 1 -> 0; matrix products, arithmetic and copies ran while one was open for 1% -> 0% of each run, Pallas kernels for 0% -> 0%
where the time goes in v1:
time: 195 us; the launch traced here: 194 us
  Pallas kernels  186 us (95%)
  local copies, waits for them, and re-layouts  8.08 us (4%)
    pallas_call x1, Pallas kernels, on_device(): pl.pallas_call(functools.partial(kernel, n), out_shape=jax.ShapeDtypeStru...  186 us
    unnamed x3, local copies, waits for them, and re-layouts  5.39 us

profile of v1, /device:TPU:0, one launch (start us, length us, event | category | flops | bytes accessed | tf_op | source)
XLA Modules:
  0.0 194.5 jit_solution(7143960503513650187)
XLA Ops:
  0.0 1.3 concatenate.3.wbias_t
  1.3 1.4 fusion
  2.7 0.7 copy.13
  3.4 0.7 copy.12
  4.1 186.4 %triangle.1 = bf16[20,640,128]{2,1,0:T(8,128)(2,1)} custom-call(bf16[20,640,128]{2,1,0:T(8,128)(2,1)} %pair.1, f32[1,128]{1,0:T(1,128)} %bitcast.10, f32[1,128]{1,0:T(1,128)} %bitcast.11, bf16[128,128]{1,0:T(8,128)(2,1)} %bitcast.8, bf16[128,128]{1,0:T(8,128)(2,1)} %get-tuple-element.7.wk, bf16[128,128]{1,0:T(8,128)(2,1)} %bitcast.7, ...), custom_call_target="tpu_custom_call" | custom-call | tf_op jit(solution)/shard_map/triangle/pallas_call | solution.py:234
  190.5 3.9 %copy.15 = bf16[20,640,128]{2,1,0:T(8,128)(2,1)} copy(bf16[20,640,128]{2,1,0:T(8,128)(2,1)} %triangle.1) | data formatting | bytes 6553600

commit v2 on v1

v2 whole, which is shorter than its diff:
```python
import functools

import jax
import jax.numpy as jnp
from jax import lax
from jax.experimental import pallas as pl
from jax.experimental.pallas import tpu as pltpu
from jax.sharding import PartitionSpec as P

HEADS = 4
HDIM = 32
CH = 128
MESH = pl.DeviceIdType.MESH
F32 = jnp.float32
BF16 = jnp.bfloat16
NT = (((1,), (1,)), ((), ()))


def normalize(values, gain, shift):
    center = jnp.mean(values, axis=-1, keepdims=True)
    spread = jnp.mean((values - center) ** 2, axis=-1, keepdims=True)
    return (values - center) * lax.rsqrt(spread + 1e-05) * gain + shift


def upper_half(shape):
    return lax.broadcasted_iota(jnp.int32, shape, len(shape) - 2) < 4


def balanced_offsets():
    rest = [(x, y, z) for x in range(4) for y in range(4) for z in range(2) if x or y or z]

    def load(o):
        out = [0] * 6
        for axis, step in enumerate((o[0], o[1], 2 * o[2])):
            out[2 * axis] += step in (1, 2)
            out[2 * axis + 1] += step in (2, 3)
        return out

    total, order = [0] * 6, []
    while rest:
        def cost(o):
            new = [t + a for t, a in zip(total, load(o))]
            return max(new) * 100 + sum(n * n for n in new), -sum(load(o))
        best = min(rest, key=cost)
        rest.remove(best)
        order.append(best)
        total = [t + a for t, a in zip(total, load(best))]
    return order


OFFSETS = balanced_offsets()


def pieces(full, size):
    return [(r, min(size, full - r)) for r in range(0, full, size)]


def interleave(*plans):
    done, out = [0] * len(plans), []
    for _ in range(sum(map(len, plans))):
        i = min(
            (i for i in range(len(plans)) if done[i] < len(plans[i])),
            key=lambda i: (done[i] + 0.5) / len(plans[i]),
        )
        out.append(plans[i][done[i]])
        done[i] += 1
    return out


def kernel(
    n, pair, gain, shift, w_qkv, wbias_t, wgate, gate_shift, wout, out_shift, out,
    send_in, recv_in, send_out, recv_out, bias_recv, bias_all,
    mix, normed, update, rows_bias, wq_t, wv_t, queries, keys, v_t, gates, scores, raised, stats, attended,
    ss_bias, rs_bias, ss_in, rs_in, ss_out, rs_out,
):
    rows, full, _ = pair.shape
    groups = send_in.shape[0]
    block = 4 * rows
    wide = n * 4
    lanes = full // CH
    units = 4 * 2 * lanes
    me = lax.axis_index("axial")
    x, y, z = me // 8, lax.rem(me // 2, 4), lax.rem(me, 2)

    def peer(o):
        return (lax.rem(x + o[0], 4) * 4 + lax.rem(y + o[1], 4)) * 2 + lax.rem(z + o[2], 2)

    barrier = pltpu.get_barrier_semaphore()
    for o in OFFSETS:
        pl.semaphore_signal(barrier, inc=1, device_id={"axial": peer(o)}, device_id_type=MESH)

    def remote(src, dst, ss, rs, to):
        return pltpu.make_async_remote_copy(
            src_ref=src, dst_ref=dst, send_sem=ss, recv_sem=rs, device_id={"axial": to}, device_id_type=MESH
        )

    def wait_bytes(ref, sem):
        pltpu.make_async_copy(ref, ref, sem).wait()

    def assemble(g):
        top = upper_half((n // 2, 8, CH))
        here = pl.ds(pl.multiple_of(g * wide, wide), wide)
        for a in range(0, rows, 2):
            even = pair[a, here, :].astype(F32).reshape(n // 2, 8, CH)
            odd = pair[a + 1, here, :].astype(F32).reshape(n // 2, 8, CH)
            mix[:, 0, 4 * a : 4 * a + 8, :] = jnp.where(top, even, pltpu.roll(odd, 4, 1))
            mix[:, 1, 4 * a : 4 * a + 8, :] = jnp.where(top, pltpu.roll(even, 4, 1), odd)
        send_in[g] = mix[...].astype(BF16).reshape(n, block, CH)

    def send_group(src, dst, ss, rs, g):
        for o in OFFSETS:
            to = peer(o)
            remote(src.at[g, to], dst.at[g, me], ss.at[g], rs.at[g], to).start()
        pltpu.make_async_copy(src.at[g, me], dst.at[g, me], rs.at[g]).start()

    assemble(0)
    pl.semaphore_wait(barrier, n - 1)
    send_group(send_in, recv_in, ss_in, rs_in, 0)

    def bias_row(k, _):
        normal = normalize(pair[k].astype(F32), gain[...], shift[...]).astype(BF16)
        line = lax.dot_general(wbias_t[...], normal, NT, preferred_element_type=F32)
        for h in range(HEADS):
            place = jnp.where(k < 16, h * 16 + k, 4 * h + 48 + k)
            rows_bias[pl.ds(place, 1), :] = line[h : h + 1, :]
        return 0

    lax.fori_loop(0, rows, bias_row, 0)
    bias_recv[x, y, z] = rows_bias[...].astype(BF16)

    first, second, third = slice(0, 32), slice(32, 64), slice(64, 80)
    every = slice(None)
    three = slice(0, 3)
    to_x = [(1, 0, 0), (3, 0, 0), (2, 0, 0)]
    to_y = [(0, 1, 0), (0, 3, 0), (0, 2, 0)]
    to_z = [(0, 0, 1)]
    waves = [
        [((x, y, z, first), to_z, (0, 0, 0, first)), ((x, y, z, second), to_x, (three, 0, 0, second)),
         ((x, y, z, third), to_y, (0, three, 0, third))],
        [((x, y, every, first), to_y, (0, three, every, first)), ((every, y, z, second), to_z, (every, 0, 0, second)),
         ((x, every, z, third), to_x, (three, every, 0, third))],
        [((x, every, every, first), to_x, (three, every, every, first)),
         ((every, y, every, second), to_y, (every, three, every, second)),
         ((every, every, z, third), to_z, (every, every, 0, third))],
    ]

    def start_wave(w):
        for p, (part, targets, _) in enumerate(waves[w]):
            for o in targets:
                remote(bias_recv.at[part], bias_recv.at[part], ss_bias.at[3 * w + p], rs_bias.at[3 * w + p], peer(o)).start()

    def wait_wave(w, sems):
        for p, (_, _, size) in enumerate(waves[w]):
            wait_bytes(bias_recv.at[size], sems.at[3 * w + p])

    start_wave(0)

    def rest(g, _):
        assemble(g)
        return 0

    lax.fori_loop(1, groups, rest, 0)
    wq_t[...] = w_qkv[:, 0:CH].astype(F32).T.astype(BF16)
    wv_t[...] = w_qkv[:, 2 * CH :].astype(F32).T.astype(BF16)
    queries[...] = jnp.zeros(queries.shape, BF16)
    wait_wave(0, rs_bias)
    start_wave(1)
    wait_wave(1, rs_bias)
    start_wave(2)

    def send_rest(g, _):
        send_group(send_in, recv_in, ss_in, rs_in, g)
        return 0

    lax.fori_loop(1, groups, send_rest, 0)

    def spread_bias(p, _):
        top = upper_half((8, full))
        turn = lambda tile: pltpu.roll(tile, 4, 0)
        px, py = p // 4, lax.rem(p, 4)
        even = bias_recv[px, py, 0].astype(F32)
        odd = bias_recv[px, py, 1].astype(F32)
        for h in range(HEADS):
            tail = slice(64 + h // 2 * 8, 72 + h // 2 * 8)
            even_tail, odd_tail = even[tail], odd[tail]
            if h % 2:
                even_tail = turn(even_tail)
            else:
                odd_tail = turn(odd_tail)
            low, high = turn(odd[16 * h : 16 * h + 8]), turn(odd[16 * h + 8 : 16 * h + 16])
            tiles = [
                even[16 * h : 16 * h + 8], even[16 * h + 8 : 16 * h + 16], jnp.where(top, even_tail, low),
                jnp.where(top, low, high), jnp.where(top, high, odd_tail),
            ]
            for k, tile in enumerate(tiles):
                start = pl.multiple_of(2 * rows * p + 8 * k, 8)
                for i in range(lanes):
                    bias_all[h // 2 * lanes + i, pl.ds(start, 8), h % 2 * CH : (h % 2 + 1) * CH] = tile[
                        :, i * CH : (i + 1) * CH
                    ]
        return 0

    def prepare(g):
        wait_bytes(recv_in.at[g], rs_in.at[g])

        def norm_block(s, _):
            values = recv_in[g, pl.ds(4 * s, 4)].astype(F32).reshape(4 * block, CH)
            normed[pl.ds(pl.multiple_of(4 * block * s, 4 * block), 4 * block), :] = normalize(
                values, gain[...], shift[...]
            )
            return 0

        lax.fori_loop(0, n // 4, norm_block, 0)

        def column(b, _):
            normal = normed[pl.ds(b, full, stride=4), :].astype(BF16)
            query = lax.dot_general(wq_t[...], normal, NT, preferred_element_type=F32)
            query = (query * HDIM ** (-0.5)).astype(BF16)
            for h in range(HEADS):
                own = slice(h * HDIM, (h + 1) * HDIM)
                for i in range(lanes):
                    queries[(b * 2 + h // 2) * lanes + i, own, h % 2 * CH : (h % 2 + 1) * CH] = query[
                        own, i * CH : (i + 1) * CH
                    ]
            keys[b] = jnp.dot(normal, w_qkv[:, CH : 2 * CH], preferred_element_type=F32).astype(BF16)
            v_t[b] = lax.dot_general(wv_t[...], normal, NT, preferred_element_type=F32).astype(BF16)
            gates[b] = jax.nn.sigmoid(jnp.dot(normal, wgate[...], preferred_element_type=F32) + gate_shift[...])
            return 0

        lax.fori_loop(0, 4, column, 0)

    plan = interleave(
        [(3, *c) for c in pieces(full, 128)], [(2, *c) for c in pieces(full, 128)], [(1, *c) for c in pieces(full, 320)]
    )

    def attend():
        def unit(t, slot):
            t1, t3 = jnp.minimum(t, units - 1), jnp.clip(t - 2, 0, units - 1)
            column1, place1 = t1 // (2 * lanes), lax.rem(t1, 2 * lanes)
            column3, place3 = t3 // (2 * lanes), lax.rem(t3, 2 * lanes)
            heads3, lane3 = pl.multiple_of(place3 // lanes * 2 * HDIM, 2 * HDIM), lax.rem(place3, lanes)
            query = queries[t1]
            top = jnp.max(stats[1 - slot, 0:8, :], axis=0, keepdims=True)
            share = 1.0 / jnp.sum(stats[slot, 8:16, :], axis=0, keepdims=True)
            most = jnp.full((8, 2 * CH), -jnp.inf, F32)
            total = jnp.zeros((8, 2 * CH), F32)
            result = jnp.zeros((2 * HDIM, 2 * CH), F32)
            for step, r, size in plan:
                here = slice(r, r + size)
                if step == 1:
                    score = jnp.dot(keys[column1, here, :], query, preferred_element_type=F32) + bias_all[place1, here, :]
                    scores[slot, here, :] = score
                    most = jnp.maximum(most, jnp.max(score.reshape(size // 8, 8, 2 * CH), axis=0))
                elif step == 2:
                    power = jnp.exp(scores[1 - slot, here, :] - top)
                    raised[1 - slot, here, :] = power
                    total = total + jnp.sum(power.reshape(size // 8, 8, 2 * CH), axis=0)
                else:
                    weights = (raised[slot, here, :] * share).astype(BF16)
                    result = result + jnp.dot(
                        v_t[column3, pl.ds(heads3, 2 * HDIM), here], weights, preferred_element_type=F32
                    )
            stats[slot, 0:8, :] = most
            stats[1 - slot, 8:16, :] = total
            attended[column3, lane3, pl.ds(heads3, HDIM), :] = result[0:HDIM, 0:CH]
            attended[column3, lane3, pl.ds(heads3 + HDIM, HDIM), :] = result[HDIM : 2 * HDIM, CH : 2 * CH]

        def two(u, _):
            unit(2 * u, 0)
            unit(2 * u + 1, 1)
            return 0

        lax.fori_loop(0, units // 2 + 1, two, 0)

    def conclude(g):
        def column(b, _):
            for i in range(lanes):
                rounded = attended[b, i].T.astype(BF16).astype(F32)
                gated = (gates[b, i * CH : (i + 1) * CH, :] * rounded).astype(BF16)
                update[pl.ds(b + 4 * CH * i, CH, stride=4), :] = (
                    jnp.dot(gated, wout[...], preferred_element_type=F32) + out_shift[...]
                )
            return 0

        lax.fori_loop(0, 4, column, 0)

        def finish(s, _):
            values = recv_in[g, pl.ds(4 * s, 4)].astype(F32)
            here = pl.ds(pl.multiple_of(4 * block * s, 4 * block), 4 * block)
            send_out[g, pl.ds(4 * s, 4)] = (update[here, :].reshape(4, block, CH) + values).astype(BF16)
            return 0

        lax.fori_loop(0, n // 4, finish, 0)
        send_group(send_out, recv_out, ss_out, rs_out, g)

    prepare(0)
    wait_wave(2, rs_bias)
    lax.fori_loop(0, n // 2, spread_bias, 0)

    def group(g, _):
        attend()
        conclude(g)

        @pl.when(g < groups - 1)
        def _():
            prepare(g + 1)

        return 0

    lax.fori_loop(0, groups, group, 0)

    def collect(g, _):
        wait_bytes(recv_out.at[g], rs_out.at[g])
        top = upper_half((n // 2, 8, CH))
        mix[...] = recv_out[g].astype(F32).reshape(n // 2, 2, block, CH)
        for a in range(0, rows, 2):
            low = mix[:, 0, 4 * a : 4 * a + 8, :]
            high = mix[:, 1, 4 * a : 4 * a + 8, :]
            even = jnp.where(top, low, pltpu.roll(high, 4, 1))
            odd = jnp.where(top, pltpu.roll(low, 4, 1), high)
            here = pl.ds(pl.multiple_of(g * wide, wide), wide)
            out[a, here, :] = even.reshape(wide, CH).astype(BF16)
            out[a + 1, here, :] = odd.reshape(wide, CH).astype(BF16)
        return 0

    lax.fori_loop(0, groups, collect, 0)

    for w in range(3):
        wait_wave(w, ss_bias)

    def drain(g, _):
        wait_bytes(send_in.at[g, pl.ds(0, n - 1)], ss_in.at[g])
        wait_bytes(send_out.at[g, pl.ds(0, n - 1)], ss_out.at[g])
        return 0

    lax.fori_loop(0, groups, drain, 0)


def on_device(n, pair_act, ln_gain, ln_shift, w_qkv, w_bias, w_gate, gate_shift, w_out, out_shift):
    rows, full, channels = pair_act.shape
    groups = full // (4 * n)
    block = 4 * rows
    lanes = full // CH
    wbias_t = jnp.concatenate([w_bias.T, jnp.zeros((16 - HEADS, channels), BF16)], axis=0)
    vmem = pl.BlockSpec(memory_space=pltpu.VMEM)
    dma = pltpu.SemaphoreType.DMA
    return pl.pallas_call(
        functools.partial(kernel, n),
        out_shape=jax.ShapeDtypeStruct(pair_act.shape, BF16),
        in_specs=[vmem] * 9,
        out_specs=vmem,
        scratch_shapes=[
            pltpu.VMEM((groups, n, block, CH), BF16),
            pltpu.VMEM((groups, n, block, CH), BF16),
            pltpu.VMEM((groups, n, block, CH), BF16),
            pltpu.VMEM((groups, n, block, CH), BF16),
            pltpu.VMEM((4, 4, 2, HEADS * rows, full), BF16),
            pltpu.VMEM((2 * lanes, full, 2 * CH), F32),
            pltpu.VMEM((n // 2, 2, block, CH), F32),
            pltpu.VMEM((n * block, CH), F32),
            pltpu.VMEM((n * block, CH), F32),
            pltpu.VMEM((HEADS * rows, full), F32),
            pltpu.VMEM((CH, CH), BF16),
            pltpu.VMEM((CH, CH), BF16),
            pltpu.VMEM((8 * lanes, CH, 2 * CH), BF16),
            pltpu.VMEM((4, full, CH), BF16),
            pltpu.VMEM((4, CH, full), BF16),
            pltpu.VMEM((4, full, CH), F32),
            pltpu.VMEM((2, full, 2 * CH), F32),
            pltpu.VMEM((2, full, 2 * CH), F32),
            pltpu.VMEM((2, 16, 2 * CH), F32),
            pltpu.VMEM((4, lanes, CH, CH), F32),
            dma((9,)), dma((9,)), dma((groups,)), dma((groups,)), dma((groups,)), dma((groups,)),
        ],
        compiler_params=pltpu.CompilerParams(
            collective_id=0, has_side_effects=True, vmem_limit_bytes=54 * 2**20
        ),
        name="triangle",
    )(
        pair_act, ln_gain[None], ln_shift[None], w_qkv, wbias_t, w_gate, gate_shift[None], w_out, out_shift[None],
    )


def solution(mesh):
    in_specs = (P(("dp", "axial"), None, None), P(), P(), P(), P(), P(), P(), P(), P())
    out_specs = P(("dp", "axial"), None, None)
    return jax.shard_map(
        functools.partial(on_device, mesh.shape["axial"]),
        mesh=mesh, in_specs=in_specs, out_specs=out_specs, check_vma=False,
    )
```

time: 195 us -> 140 us (0.72)
  Pallas kernels: 186 us -> 134 us
  local copies, waits for them, and re-layouts: 8.08 us -> 5.22 us
    pallas_call x1, Pallas kernels: 186 us -> 134 us  [on_device(): pl.pallas_call(functools.partial(kernel, n), out_shape=jax.ShapeDtypeStru...]
    unnamed x3 -> x1, local copies, waits for them, and re-layouts: 5.39 us -> 3.95 us
where the time goes in v2:
time: 140 us; the launch traced here: 139 us
  Pallas kernels  134 us (96%)
  local copies, waits for them, and re-layouts  5.22 us (4%)
    pallas_call x1, Pallas kernels, on_device(): pl.pallas_call(functools.partial(kernel, n), out_shape=jax.ShapeDtypeStru...  134 us
    unnamed x1, local copies, waits for them, and re-layouts  3.95 us

profile of v2, /device:TPU:0, one launch (start us, length us, event | category | flops | bytes accessed | tf_op | source)
XLA Modules:
  0.0 139.2 jit_solution(17110840232233005321)
XLA Ops:
  0.0 1.3 concatenate.3.wbias_t
  1.3 133.9 %triangle.1 = bf16[20,640,128]{2,1,0:T(8,128)(2,1)} custom-call(bf16[20,640,128]{2,1,0:T(8,128)(2,1)} %pair.1, f32[1,128]{1,0:T(1,128)} %bitcast.6, f32[1,128]{1,0:T(1,128)} %bitcast.7, bf16[128,384]{1,0:T(8,128)(2,1)} %w_qkv.1, bf16[16,128]{1,0:T(8,128)(2,1)} %concatenate.3.wbias_t, bf16[128,128]{1,0:T(8,128)(2,1)} %wgate.1, f32[1,128]{1,0:T(1,128)} %bitcast.8, ...), custom_call_target="tpu_custom_call" | custom-call | tf_op jit(solution)/shard_map/triangle/pallas_call | solution.py:347
  135.2 3.9 %copy.11 = bf16[20,640,128]{2,1,0:T(8,128)(2,1)} copy(bf16[20,640,128]{2,1,0:T(8,128)(2,1)} %triangle.1) | data formatting | bytes 6553600

commit v3 on v2

--- a/solution.py
+++ b/solution.py
@@ -10,6 +10,7 @@
 HEADS = 4
 HDIM = 32
 CH = 128
+LOG2E = 1.4426950408889634
 MESH = pl.DeviceIdType.MESH
 F32 = jnp.float32
 BF16 = jnp.bfloat16
@@ -68,9 +69,9 @@
 
 
 def kernel(
-    n, pair, gain, shift, w_qkv, wbias_t, wgate, gate_shift, wout, out_shift, out,
+    n, pair, gain, shift, w_qkv, w_bias, wgate, gate_shift, wout, out_shift, out,
     send_in, recv_in, send_out, recv_out, bias_recv, bias_all,
-    mix, normed, update, rows_bias, wq_t, wv_t, queries, keys, v_t, gates, scores, raised, stats, attended,
+    mix, normed, update, rows_bias, wq_t, wk_twice, wv_t, queries, keys, v_t, gates, scores, raised, stats, attended,
     ss_bias, rs_bias, ss_in, rs_in, ss_out, rs_out,
 ):
     rows, full, _ = pair.shape
@@ -94,6 +95,9 @@
             src_ref=src, dst_ref=dst, send_sem=ss, recv_sem=rs, device_id={"axial": to}, device_id_type=MESH
         )
 
+    def chunk(d):
+        return pl.ds(pl.multiple_of(d * block, block), block)
+
     def wait_bytes(ref, sem):
         pltpu.make_async_copy(ref, ref, sem).wait()
 
@@ -105,27 +109,26 @@
             odd = pair[a + 1, here, :].astype(F32).reshape(n // 2, 8, CH)
             mix[:, 0, 4 * a : 4 * a + 8, :] = jnp.where(top, even, pltpu.roll(odd, 4, 1))
             mix[:, 1, 4 * a : 4 * a + 8, :] = jnp.where(top, pltpu.roll(even, 4, 1), odd)
-        send_in[g] = mix[...].astype(BF16).reshape(n, block, CH)
+        send_in[g] = mix[...].astype(BF16).reshape(n * block, CH)
 
     def send_group(src, dst, ss, rs, g):
         for o in OFFSETS:
             to = peer(o)
-            remote(src.at[g, to], dst.at[g, me], ss.at[g], rs.at[g], to).start()
-        pltpu.make_async_copy(src.at[g, me], dst.at[g, me], rs.at[g]).start()
-
-    assemble(0)
-    pl.semaphore_wait(barrier, n - 1)
-    send_group(send_in, recv_in, ss_in, rs_in, 0)
-
-    def bias_row(k, _):
-        normal = normalize(pair[k].astype(F32), gain[...], shift[...]).astype(BF16)
-        line = lax.dot_general(wbias_t[...], normal, NT, preferred_element_type=F32)
-        for h in range(HEADS):
-            place = jnp.where(k < 16, h * 16 + k, 4 * h + 48 + k)
-            rows_bias[pl.ds(place, 1), :] = line[h : h + 1, :]
-        return 0
-
-    lax.fori_loop(0, rows, bias_row, 0)
+            remote(src.at[g, chunk(to)], dst.at[g, chunk(me)], ss.at[g], rs.at[g], to).start()
+        pltpu.make_async_copy(src.at[g, chunk(me)], dst.at[g, chunk(me)], rs.at[g]).start()
+
+    wbias_t = w_bias[...]
+
+    def bias_rows(k4, _):
+        for k in range(4):
+            normal = normalize(pair[4 * k4 + k].astype(F32), gain[...], shift[...]).astype(BF16)
+            line = lax.dot_general(wbias_t, normal, NT, preferred_element_type=F32)
+            for h in range(HEADS):
+                place = jnp.where(k4 < 4, h * 16 + 4 * k4, 4 * h + 64) + k
+                rows_bias[pl.ds(place, 1), :] = line[h : h + 1, :]
+        return 0
+
+    lax.fori_loop(0, rows // 4, bias_rows, 0)
     bias_recv[x, y, z] = rows_bias[...].astype(BF16)
 
     first, second, third = slice(0, 32), slice(32, 64), slice(64, 80)
@@ -153,7 +156,10 @@
         for p, (_, _, size) in enumerate(waves[w]):
             wait_bytes(bias_recv.at[size], sems.at[3 * w + p])
 
+    pl.semaphore_wait(barrier, n - 1)
     start_wave(0)
+    assemble(0)
+    send_group(send_in, recv_in, ss_in, rs_in, 0)
 
     def rest(g, _):
         assemble(g)
@@ -161,6 +167,11 @@
 
     lax.fori_loop(1, groups, rest, 0)
     wq_t[...] = w_qkv[:, 0:CH].astype(F32).T.astype(BF16)
+    wk = w_qkv[:, CH : 2 * CH].astype(F32)
+    swapped = pltpu.roll(wk, 2 * HDIM, 1)
+    left = lax.broadcasted_iota(jnp.int32, (CH, CH), 1) < 2 * HDIM
+    wk_twice[0] = jnp.where(left, wk, swapped).astype(BF16)
+    wk_twice[1] = jnp.where(left, swapped, wk).astype(BF16)
     wv_t[...] = w_qkv[:, 2 * CH :].astype(F32).T.astype(BF16)
     queries[...] = jnp.zeros(queries.shape, BF16)
     wait_wave(0, rs_bias)
@@ -178,8 +189,8 @@
         top = upper_half((8, full))
         turn = lambda tile: pltpu.roll(tile, 4, 0)
         px, py = p // 4, lax.rem(p, 4)
-        even = bias_recv[px, py, 0].astype(F32)
-        odd = bias_recv[px, py, 1].astype(F32)
+        even = bias_recv[px, py, 0].astype(F32) * LOG2E
+        odd = bias_recv[px, py, 1].astype(F32) * LOG2E
         for h in range(HEADS):
             tail = slice(64 + h // 2 * 8, 72 + h // 2 * 8)
             even_tail, odd_tail = even[tail], odd[tail]
@@ -204,42 +215,52 @@
         wait_bytes(recv_in.at[g], rs_in.at[g])
 
         def norm_block(s, _):
-            values = recv_in[g, pl.ds(4 * s, 4)].astype(F32).reshape(4 * block, CH)
-            normed[pl.ds(pl.multiple_of(4 * block * s, 4 * block), 4 * block), :] = normalize(
-                values, gain[...], shift[...]
-            )
+            here = pl.ds(pl.multiple_of(8 * block * s, 8 * block), 8 * block)
+            normed[here, :] = normalize(recv_in[g, here, :].astype(F32), gain[...], shift[...])
             return 0
 
-        lax.fori_loop(0, n // 4, norm_block, 0)
-
-        def column(b, _):
+        lax.fori_loop(0, n // 8, norm_block, 0)
+
+        def column(b):
             normal = normed[pl.ds(b, full, stride=4), :].astype(BF16)
             query = lax.dot_general(wq_t[...], normal, NT, preferred_element_type=F32)
-            query = (query * HDIM ** (-0.5)).astype(BF16)
+            query = (query * HDIM ** (-0.5)).astype(BF16).astype(F32) * LOG2E
+            high = query.astype(BF16)
+            low = (query - high.astype(F32)).astype(BF16)
             for h in range(HEADS):
                 own = slice(h * HDIM, (h + 1) * HDIM)
                 for i in range(lanes):
-                    queries[(b * 2 + h // 2) * lanes + i, own, h % 2 * CH : (h % 2 + 1) * CH] = query[
-                        own, i * CH : (i + 1) * CH
-                    ]
-            keys[b] = jnp.dot(normal, w_qkv[:, CH : 2 * CH], preferred_element_type=F32).astype(BF16)
+                    unit, side, here = (b * 2 + h // 2) * lanes + i, h % 2 * CH, slice(i * CH, (i + 1) * CH)
+                    row = h % 2 * HDIM
+                    queries[unit, row : row + HDIM, side : side + CH] = high[own, here]
+                    queries[unit, 2 * HDIM + row : 3 * HDIM + row, side : side + CH] = low[own, here]
+            for p in range(2):
+                keys[b, p] = jnp.dot(normal, wk_twice[p], preferred_element_type=F32).astype(BF16)
             v_t[b] = lax.dot_general(wv_t[...], normal, NT, preferred_element_type=F32).astype(BF16)
             gates[b] = jax.nn.sigmoid(jnp.dot(normal, wgate[...], preferred_element_type=F32) + gate_shift[...])
+
+        def columns(b2, _):
+            column(2 * b2)
+            column(2 * b2 + 1)
             return 0
 
-        lax.fori_loop(0, 4, column, 0)
+        lax.fori_loop(0, 2, columns, 0)
 
     plan = interleave(
         [(3, *c) for c in pieces(full, 128)], [(2, *c) for c in pieces(full, 128)], [(1, *c) for c in pieces(full, 320)]
     )
 
-    def attend():
+    def query_block(turn):
+        return lax.rem(turn + me, lanes)
+
+    def attend(g):
         def unit(t, slot):
             t1, t3 = jnp.minimum(t, units - 1), jnp.clip(t - 2, 0, units - 1)
-            column1, place1 = t1 // (2 * lanes), lax.rem(t1, 2 * lanes)
-            column3, place3 = t3 // (2 * lanes), lax.rem(t3, 2 * lanes)
-            heads3, lane3 = pl.multiple_of(place3 // lanes * 2 * HDIM, 2 * HDIM), lax.rem(place3, lanes)
-            query = queries[t1]
+            column1, heads1 = lax.rem(t1, 8) // 2, lax.rem(t1, 2)
+            place1 = heads1 * lanes + query_block(t1 // 8)
+            column3, lane3 = lax.rem(t3, 8) // 2, query_block(t3 // 8)
+            heads3 = pl.multiple_of(lax.rem(t3, 2) * 2 * HDIM, 2 * HDIM)
+            query = queries[column1 * 2 * lanes + place1]
             top = jnp.max(stats[1 - slot, 0:8, :], axis=0, keepdims=True)
             share = 1.0 / jnp.sum(stats[slot, 8:16, :], axis=0, keepdims=True)
             most = jnp.full((8, 2 * CH), -jnp.inf, F32)
@@ -248,11 +269,11 @@
             for step, r, size in plan:
                 here = slice(r, r + size)
                 if step == 1:
-                    score = jnp.dot(keys[column1, here, :], query, preferred_element_type=F32) + bias_all[place1, here, :]
+                    score = jnp.dot(keys[column1, heads1, here, :], query, preferred_element_type=F32) + bias_all[place1, here, :]
                     scores[slot, here, :] = score
                     most = jnp.maximum(most, jnp.max(score.reshape(size // 8, 8, 2 * CH), axis=0))
                 elif step == 2:
-                    power = jnp.exp(scores[1 - slot, here, :] - top)
+                    power = jnp.exp2(scores[1 - slot, here, :] - top)
                     raised[1 - slot, here, :] = power
                     total = total + jnp.sum(power.reshape(size // 8, 8, 2 * CH), axis=0)
                 else:
@@ -270,36 +291,52 @@
             unit(2 * u + 1, 1)
             return 0
 
-        lax.fori_loop(0, units // 2 + 1, two, 0)
-
-    def conclude(g):
-        def column(b, _):
-            for i in range(lanes):
-                rounded = attended[b, i].T.astype(BF16).astype(F32)
-                gated = (gates[b, i * CH : (i + 1) * CH, :] * rounded).astype(BF16)
-                update[pl.ds(b + 4 * CH * i, CH, stride=4), :] = (
-                    jnp.dot(gated, wout[...], preferred_element_type=F32) + out_shift[...]
-                )
+        def turn(i, _):
+            two(4 * i, 0)
+
+            @pl.when(i > 0)
+            def _():
+                conclude(g, i - 1)
+
+            @pl.when(i < lanes)
+            def _():
+                lax.fori_loop(4 * i + 1, 4 * i + 4, two, 0)
+
             return 0
 
-        lax.fori_loop(0, 4, column, 0)
-
-        def finish(s, _):
-            values = recv_in[g, pl.ds(4 * s, 4)].astype(F32)
-            here = pl.ds(pl.multiple_of(4 * block * s, 4 * block), 4 * block)
-            send_out[g, pl.ds(4 * s, 4)] = (update[here, :].reshape(4, block, CH) + values).astype(BF16)
+        lax.fori_loop(0, lanes + 1, turn, 0)
+
+    def conclude(g, turn):
+        i = query_block(turn)
+
+        for b in range(4):
+            rounded = attended[b, i].T.astype(BF16).astype(F32)
+            gated = (gates[b, pl.ds(pl.multiple_of(i * CH, CH), CH), :] * rounded).astype(BF16)
+            update[pl.ds(b, CH, stride=4), :] = jnp.dot(gated, wout[...], preferred_element_type=F32) + out_shift[...]
+        here = pl.ds(pl.multiple_of(4 * CH * i, 4 * CH), 4 * CH)
+        send_out[g, here, :] = (update[...] + recv_in[g, here, :].astype(F32)).astype(BF16)
+
+        def give(s, _):
+            @pl.when(s != me)
+            def _():
+                remote(send_out.at[g, chunk(s)], recv_out.at[g, chunk(me)], ss_out.at[g], rs_out.at[g], s).start()
+
+            @pl.when(s == me)
+            def _():
+                pltpu.make_async_copy(send_out.at[g, chunk(s)], recv_out.at[g, chunk(s)], rs_out.at[g]).start()
+
             return 0
 
-        lax.fori_loop(0, n // 4, finish, 0)
-        send_group(send_out, recv_out, ss_out, rs_out, g)
+        least = (CH * i + rows - 1) // rows - jnp.where((turn > 0) & (i > 0), 1, 0)
+        most = CH * (i + 1) // rows + jnp.where((turn == lanes - 1) & (i < lanes - 1), 1, 0)
+        lax.fori_loop(least, most, give, 0)
 
     prepare(0)
     wait_wave(2, rs_bias)
     lax.fori_loop(0, n // 2, spread_bias, 0)
 
     def group(g, _):
-        attend()
-        conclude(g)
+        attend(g)
 
         @pl.when(g < groups - 1)
         def _():
@@ -329,8 +366,8 @@
         wait_wave(w, ss_bias)
 
     def drain(g, _):
-        wait_bytes(send_in.at[g, pl.ds(0, n - 1)], ss_in.at[g])
-        wait_bytes(send_out.at[g, pl.ds(0, n - 1)], ss_out.at[g])
+        wait_bytes(send_in.at[g, pl.ds(0, (n - 1) * block)], ss_in.at[g])
+        wait_bytes(send_out.at[g, pl.ds(0, (n - 1) * block)], ss_out.at[g])
         return 0
 
     lax.fori_loop(0, groups, drain, 0)
@@ -341,7 +378,6 @@
     groups = full // (4 * n)
     block = 4 * rows
     lanes = full // CH
-    wbias_t = jnp.concatenate([w_bias.T, jnp.zeros((16 - HEADS, channels), BF16)], axis=0)
     vmem = pl.BlockSpec(memory_space=pltpu.VMEM)
     dma = pltpu.SemaphoreType.DMA
     return pl.pallas_call(
@@ -350,20 +386,21 @@
         in_specs=[vmem] * 9,
         out_specs=vmem,
         scratch_shapes=[
-            pltpu.VMEM((groups, n, block, CH), BF16),
-            pltpu.VMEM((groups, n, block, CH), BF16),
-            pltpu.VMEM((groups, n, block, CH), BF16),
-            pltpu.VMEM((groups, n, block, CH), BF16),
+            pltpu.VMEM((groups, n * block, CH), BF16),
+            pltpu.VMEM((groups, n * block, CH), BF16),
+            pltpu.VMEM((groups, n * block, CH), BF16),
+            pltpu.VMEM((groups, n * block, CH), BF16),
             pltpu.VMEM((4, 4, 2, HEADS * rows, full), BF16),
             pltpu.VMEM((2 * lanes, full, 2 * CH), F32),
             pltpu.VMEM((n // 2, 2, block, CH), F32),
             pltpu.VMEM((n * block, CH), F32),
-            pltpu.VMEM((n * block, CH), F32),
+            pltpu.VMEM((4 * CH, CH), F32),
             pltpu.VMEM((HEADS * rows, full), F32),
             pltpu.VMEM((CH, CH), BF16),
+            pltpu.VMEM((2, CH, CH), BF16),
             pltpu.VMEM((CH, CH), BF16),
             pltpu.VMEM((8 * lanes, CH, 2 * CH), BF16),
-            pltpu.VMEM((4, full, CH), BF16),
+            pltpu.VMEM((4, 2, full, CH), BF16),
             pltpu.VMEM((4, CH, full), BF16),
             pltpu.VMEM((4, full, CH), F32),
             pltpu.VMEM((2, full, 2 * CH), F32),
@@ -373,11 +410,11 @@
             dma((9,)), dma((9,)), dma((groups,)), dma((groups,)), dma((groups,)), dma((groups,)),
         ],
         compiler_params=pltpu.CompilerParams(
-            collective_id=0, has_side_effects=True, vmem_limit_bytes=54 * 2**20
+            collective_id=0, has_side_effects=True, vmem_limit_bytes=56 * 2**20
         ),
         name="triangle",
     )(
-        pair_act, ln_gain[None], ln_shift[None], w_qkv, wbias_t, w_gate, gate_shift[None], w_out, out_shift[None],
+        pair_act, ln_gain[None], ln_shift[None], w_qkv, w_bias.T, w_gate, gate_shift[None], w_out, out_shift[None],
     )
 
 

time: 140 us -> 131 us (0.936)
  Pallas kernels: 134 us -> 126 us
    pallas_call x1, Pallas kernels: 134 us -> 126 us  [on_device(): pl.pallas_call(functools.partial(kernel, n), out_shape=jax.ShapeDtypeStru...]
where the time goes in v3:
time: 131 us; the launch traced here: 130 us
  Pallas kernels  126 us (96%)
  local copies, waits for them, and re-layouts  3.95 us (3%)
    pallas_call x1, Pallas kernels, on_device(): pl.pallas_call(functools.partial(kernel, n), out_shape=jax.ShapeDtypeStru...  126 us
    unnamed x1, local copies, waits for them, and re-layouts  3.95 us

profile of v3, /device:TPU:0, one launch (start us, length us, event | category | flops | bytes accessed | tf_op | source)
XLA Modules:
  0.0 130.4 jit_solution(16358926806785113407)
XLA Ops:
  0.0 126.4 %triangle.1 = bf16[20,640,128]{2,1,0:T(8,128)(2,1)} custom-call(bf16[20,640,128]{2,1,0:T(8,128)(2,1)} %pair.1, f32[1,128]{1,0:T(1,128)} %bitcast.6, f32[1,128]{1,0:T(1,128)} %bitcast.7, bf16[128,384]{1,0:T(8,128)(2,1)} %w_qkv.1, bf16[4,128]{1,0:T(4,128)(2,1)} %bitcast.5, bf16[128,128]{1,0:T(8,128)(2,1)} %wgate.1, f32[1,128]{1,0:T(1,128)} %bitcast.8, ...), custom_call_target="tpu_custom_call" | custom-call | tf_op jit(solution)/shard_map/triangle/pallas_call | solution.py:383
  126.4 3.9 %copy.11 = bf16[20,640,128]{2,1,0:T(8,128)(2,1)} copy(bf16[20,640,128]{2,1,0:T(8,128)(2,1)} %triangle.1) | data formatting | bytes 6553600

commit v4 on v3

--- a/solution.py
+++ b/solution.py
@@ -69,8 +69,8 @@
 
 
 def kernel(
-    n, pair, gain, shift, w_qkv, w_bias, wgate, gate_shift, wout, out_shift, out,
-    send_in, recv_in, send_out, recv_out, bias_recv, bias_all,
+    n, pair, gain, shift, w_qkv, w_bias, wgate, gate_shift, wout, out_shift, recv_out,
+    send_in, recv_in, send_out, bias_recv, bias_all,
     mix, normed, update, rows_bias, wq_t, wk_twice, wv_t, queries, keys, v_t, gates, scores, raised, stats, attended,
     ss_bias, rs_bias, ss_in, rs_in, ss_out, rs_out,
 ):
@@ -134,6 +134,9 @@
     first, second, third = slice(0, 32), slice(32, 64), slice(64, 80)
     every = slice(None)
     three = slice(0, 3)
+    lower, upper = slice(0, 2), slice(2, 4)
+    before = lambda place: lax.rem(place + 3, 4)
+    after = lambda place: lax.rem(place + 1, 4)
     to_x = [(1, 0, 0), (3, 0, 0), (2, 0, 0)]
     to_y = [(0, 1, 0), (0, 3, 0), (0, 2, 0)]
     to_z = [(0, 0, 1)]
@@ -142,19 +145,23 @@
          ((x, y, z, third), to_y, (0, three, 0, third))],
         [((x, y, every, first), to_y, (0, three, every, first)), ((every, y, z, second), to_z, (every, 0, 0, second)),
          ((x, every, z, third), to_x, (three, every, 0, third))],
-        [((x, every, every, first), to_x, (three, every, every, first)),
-         ((every, y, every, second), to_y, (every, three, every, second)),
+        [((x, every, every, first), to_x[:2], (lower, every, every, first)),
+         ((every, y, every, second), to_y[:2], (every, lower, every, second)),
          ((every, every, z, third), to_z, (every, every, 0, third))],
+        [((before(x), lower, every, first), to_x[:1], (0, lower, every, first)),
+         ((after(x), upper, every, first), to_x[1:2], (0, lower, every, first)),
+         ((lower, before(y), every, second), to_y[:1], (lower, 0, every, second)),
+         ((upper, after(y), every, second), to_y[1:2], (lower, 0, every, second))],
     ]
 
     def start_wave(w):
         for p, (part, targets, _) in enumerate(waves[w]):
             for o in targets:
-                remote(bias_recv.at[part], bias_recv.at[part], ss_bias.at[3 * w + p], rs_bias.at[3 * w + p], peer(o)).start()
+                remote(bias_recv.at[part], bias_recv.at[part], ss_bias.at[4 * w + p], rs_bias.at[4 * w + p], peer(o)).start()
 
     def wait_wave(w, sems):
         for p, (_, _, size) in enumerate(waves[w]):
-            wait_bytes(bias_recv.at[size], sems.at[3 * w + p])
+            wait_bytes(bias_recv.at[size], sems.at[4 * w + p])
 
     pl.semaphore_wait(barrier, n - 1)
     start_wave(0)
@@ -182,8 +189,6 @@
     def send_rest(g, _):
         send_group(send_in, recv_in, ss_in, rs_in, g)
         return 0
-
-    lax.fori_loop(1, groups, send_rest, 0)
 
     def spread_bias(p, _):
         top = upper_half((8, full))
@@ -316,23 +321,24 @@
         here = pl.ds(pl.multiple_of(4 * CH * i, 4 * CH), 4 * CH)
         send_out[g, here, :] = (update[...] + recv_in[g, here, :].astype(F32)).astype(BF16)
 
-        def give(s, _):
-            @pl.when(s != me)
-            def _():
-                remote(send_out.at[g, chunk(s)], recv_out.at[g, chunk(me)], ss_out.at[g], rs_out.at[g], s).start()
-
-            @pl.when(s == me)
-            def _():
-                pltpu.make_async_copy(send_out.at[g, chunk(s)], recv_out.at[g, chunk(s)], rs_out.at[g]).start()
-
+        def give(j, _):
+            s = j + jnp.where(j >= me, 1, 0)
+            remote(send_out.at[g, chunk(s)], recv_out.at[g, chunk(me)], ss_out.at[g], rs_out.at[g], s).start()
             return 0
 
         least = (CH * i + rows - 1) // rows - jnp.where((turn > 0) & (i > 0), 1, 0)
         most = CH * (i + 1) // rows + jnp.where((turn == lanes - 1) & (i < lanes - 1), 1, 0)
-        lax.fori_loop(least, most, give, 0)
-
+        lax.fori_loop(least - jnp.where(least > me, 1, 0), most - jnp.where(most > me, 1, 0), give, 0)
+
+        @pl.when((least <= me) & (me < most))
+        def _():
+            pltpu.make_async_copy(send_out.at[g, chunk(me)], recv_out.at[g, chunk(me)], rs_out.at[g]).start()
+
+    wait_wave(2, rs_bias)
+    start_wave(3)
     prepare(0)
-    wait_wave(2, rs_bias)
+    wait_wave(3, rs_bias)
+    lax.fori_loop(1, groups, send_rest, 0)
     lax.fori_loop(0, n // 2, spread_bias, 0)
 
     def group(g, _):
@@ -346,31 +352,27 @@
 
     lax.fori_loop(0, groups, group, 0)
 
-    def collect(g, _):
+    for w in range(4):
+        wait_wave(w, ss_bias)
+
+    def drain(g, _):
         wait_bytes(recv_out.at[g], rs_out.at[g])
-        top = upper_half((n // 2, 8, CH))
-        mix[...] = recv_out[g].astype(F32).reshape(n // 2, 2, block, CH)
-        for a in range(0, rows, 2):
-            low = mix[:, 0, 4 * a : 4 * a + 8, :]
-            high = mix[:, 1, 4 * a : 4 * a + 8, :]
-            even = jnp.where(top, low, pltpu.roll(high, 4, 1))
-            odd = jnp.where(top, pltpu.roll(low, 4, 1), high)
-            here = pl.ds(pl.multiple_of(g * wide, wide), wide)
-            out[a, here, :] = even.reshape(wide, CH).astype(BF16)
-            out[a + 1, here, :] = odd.reshape(wide, CH).astype(BF16)
-        return 0
-
-    lax.fori_loop(0, groups, collect, 0)
-
-    for w in range(3):
-        wait_wave(w, ss_bias)
-
-    def drain(g, _):
         wait_bytes(send_in.at[g, pl.ds(0, (n - 1) * block)], ss_in.at[g])
         wait_bytes(send_out.at[g, pl.ds(0, (n - 1) * block)], ss_out.at[g])
         return 0
 
     lax.fori_loop(0, groups, drain, 0)
+
+
+def collect(received, out, mix):
+    rows, wide, _ = out.shape
+    top = upper_half((wide // 8, 8, CH))
+    mix[...] = received[0].astype(F32).reshape(mix.shape)
+    for a in range(0, rows, 2):
+        low = mix[:, 0, 4 * a : 4 * a + 8, :]
+        high = mix[:, 1, 4 * a : 4 * a + 8, :]
+        out[a] = jnp.where(top, low, pltpu.roll(high, 4, 1)).reshape(wide, CH).astype(BF16)
+        out[a + 1] = jnp.where(top, pltpu.roll(low, 4, 1), high).reshape(wide, CH).astype(BF16)
 
 
 def on_device(n, pair_act, ln_gain, ln_shift, w_qkv, w_bias, w_gate, gate_shift, w_out, out_shift):
@@ -380,13 +382,12 @@
     lanes = full // CH
     vmem = pl.BlockSpec(memory_space=pltpu.VMEM)
     dma = pltpu.SemaphoreType.DMA
-    return pl.pallas_call(
+    received = pl.pallas_call(
         functools.partial(kernel, n),
-        out_shape=jax.ShapeDtypeStruct(pair_act.shape, BF16),
+        out_shape=jax.ShapeDtypeStruct((groups, n * block, CH), BF16),
         in_specs=[vmem] * 9,
-        out_specs=vmem,
+        out_specs=pl.BlockSpec(memory_space=pl.ANY),
         scratch_shapes=[
-            pltpu.VMEM((groups, n * block, CH), BF16),
             pltpu.VMEM((groups, n * block, CH), BF16),
             pltpu.VMEM((groups, n * block, CH), BF16),
             pltpu.VMEM((groups, n * block, CH), BF16),
@@ -407,7 +408,7 @@
             pltpu.VMEM((2, full, 2 * CH), F32),
             pltpu.VMEM((2, 16, 2 * CH), F32),
             pltpu.VMEM((4, lanes, CH, CH), F32),
-            dma((9,)), dma((9,)), dma((groups,)), dma((groups,)), dma((groups,)), dma((groups,)),
+            dma((16,)), dma((16,)), dma((groups,)), dma((groups,)), dma((groups,)), dma((groups,)),
         ],
         compiler_params=pltpu.CompilerParams(
             collective_id=0, has_side_effects=True, vmem_limit_bytes=56 * 2**20
@@ -416,6 +417,16 @@
     )(
         pair_act, ln_gain[None], ln_shift[None], w_qkv, w_bias.T, w_gate, gate_shift[None], w_out, out_shift[None],
     )
+    return pl.pallas_call(
+        collect,
+        grid=(groups,),
+        out_shape=jax.ShapeDtypeStruct(pair_act.shape, BF16),
+        in_specs=[pl.BlockSpec((1, n * block, CH), lambda g: (g, 0, 0))],
+        out_specs=pl.BlockSpec((rows, 4 * n, CH), lambda g: (0, g, 0)),
+        scratch_shapes=[pltpu.VMEM((n // 2, 2, block, CH), F32)],
+        compiler_params=pltpu.CompilerParams(vmem_limit_bytes=60 * 2**20),
+        name="collect",
+    )(received)
 
 
 def solution(mesh):

time: 131 us -> 122 us (0.931)
  Pallas kernels: 126 us -> 121 us
  local copies, waits for them, and re-layouts: 3.95 us -> 0 us
    pallas_call x1, Pallas kernels: 126 us -> 116 us  [on_device(): pl.pallas_call(functools.partial(kernel, n), out_shape=jax.ShapeDtypeStru...]
    pallas_call x0 -> x1, Pallas kernels: none -> 5.48 us  [on_device(): pl.pallas_call(collect, grid=(groups,), out_shape=jax.ShapeDtypeStruct(pa...]
    unnamed x1 -> x0, local copies, waits for them, and re-layouts: 3.95 us -> none
where the time goes in v4:
time: 122 us; the launch traced here: 121 us
  Pallas kernels  121 us (99%)
    pallas_call x1, Pallas kernels, on_device(): pl.pallas_call(functools.partial(kernel, n), out_shape=jax.ShapeDtypeStru...  116 us
    pallas_call x1, Pallas kernels, on_device(): pl.pallas_call(collect, grid=(groups,), out_shape=jax.ShapeDtypeStruct(pa...  5.48 us

profile of v4, /device:TPU:0, one launch (start us, length us, event | category | flops | bytes accessed | tf_op | source)
XLA Modules:
  0.0 121.3 jit_solution(12079848339661027123)
XLA Ops:
  0.0 115.8 %triangle.1.received = bf16[5,2560,128]{2,1,0:T(8,128)(2,1)} custom-call(bf16[20,640,128]{2,1,0:T(8,128)(2,1)} %pair.1, f32[1,128]{1,0:T(1,128)} %bitcast.6, f32[1,128]{1,0:T(1,128)} %bitcast.7, bf16[128,384]{1,0:T(8,128)(2,1)} %w_qkv.1, bf16[4,128]{1,0:T(4,128)(2,1)} %bitcast.5, bf16[128,128]{1,0:T(8,128)(2,1)} %wgate.1, f32[1,128]{1,0:T(1,128)} %bitcast.8, ...), custom_call_target="tpu_custom_call" | custom-call | tf_op jit(solution)/shard_map/triangle/pallas_call | solution.py:385
  115.9 5.5 %collect.1 = bf16[20,640,128]{2,1,0:T(8,128)(2,1)} custom-call(bf16[5,2560,128]{2,1,0:T(8,128)(2,1)} %triangle.1.received), custom_call_target="tpu_custom_call" | custom-call | tf_op jit(solution)/shard_map/collect/pallas_call | solution.py:420

commit v5 on v4

--- a/solution.py
+++ b/solution.py
@@ -166,7 +166,6 @@
     pl.semaphore_wait(barrier, n - 1)
     start_wave(0)
     assemble(0)
-    send_group(send_in, recv_in, ss_in, rs_in, 0)
 
     def rest(g, _):
         assemble(g)
@@ -183,6 +182,7 @@
     queries[...] = jnp.zeros(queries.shape, BF16)
     wait_wave(0, rs_bias)
     start_wave(1)
+    send_group(send_in, recv_in, ss_in, rs_in, 0)
     wait_wave(1, rs_bias)
     start_wave(2)
 
@@ -252,7 +252,7 @@
         lax.fori_loop(0, 2, columns, 0)
 
     plan = interleave(
-        [(3, *c) for c in pieces(full, 128)], [(2, *c) for c in pieces(full, 128)], [(1, *c) for c in pieces(full, 320)]
+        [(1, *c) for c in pieces(full, 320)], [(2, *c) for c in pieces(full, 128)], [(3, *c) for c in pieces(full, 256)]
     )
 
     def query_block(turn):

time: 122 us -> 122 us (level)
  no operation moved by 1% of the time
where the time goes in v5:
time: 122 us
  Pallas kernels  121 us (99%)
    pallas_call x1, Pallas kernels, on_device(): pl.pallas_call(functools.partial(kernel, n), out_shape=jax.ShapeDtypeStru...  116 us
    pallas_call x1, Pallas kernels, on_device(): pl.pallas_call(collect, grid=(groups,), out_shape=jax.ShapeDtypeStruct(pa...  5.48 us

profile of v5, /device:TPU:0, one launch (start us, length us, event | category | flops | bytes accessed | tf_op | source)
XLA Modules:
  0.0 121.5 jit_solution(558545978284626771)
XLA Ops:
  0.0 116.0 %triangle.1.received = bf16[5,2560,128]{2,1,0:T(8,128)(2,1)} custom-call(bf16[20,640,128]{2,1,0:T(8,128)(2,1)} %pair.1, f32[1,128]{1,0:T(1,128)} %bitcast.6, f32[1,128]{1,0:T(1,128)} %bitcast.7, bf16[128,384]{1,0:T(8,128)(2,1)} %w_qkv.1, bf16[4,128]{1,0:T(4,128)(2,1)} %bitcast.5, bf16[128,128]{1,0:T(8,128)(2,1)} %wgate.1, f32[1,128]{1,0:T(1,128)} %bitcast.8, ...), custom_call_target="tpu_custom_call" | custom-call | tf_op jit(solution)/shard_map/triangle/pallas_call | solution.py:385
  116.0 5.5 %collect.1 = bf16[20,640,128]{2,1,0:T(8,128)(2,1)} custom-call(bf16[5,2560,128]{2,1,0:T(8,128)(2,1)} %triangle.1.received), custom_call_target="tpu_custom_call" | custom-call | tf_op jit(solution)/shard_map/collect/pallas_call | solution.py:420

commit v6 on v5

--- a/solution.py
+++ b/solution.py
@@ -339,7 +339,12 @@
     prepare(0)
     wait_wave(3, rs_bias)
     lax.fori_loop(1, groups, send_rest, 0)
-    lax.fori_loop(0, n // 2, spread_bias, 0)
+    def spread_two(p2, _):
+        spread_bias(2 * p2, 0)
+        spread_bias(2 * p2 + 1, 0)
+        return 0
+
+    lax.fori_loop(0, n // 4, spread_two, 0)
 
     def group(g, _):
         attend(g)

time: 122 us -> 122 us (level)
  no operation moved by 1% of the time
where the time goes in v6:
time: 122 us; the launch traced here: 121 us
  Pallas kernels  121 us (99%)
    pallas_call x1, Pallas kernels, on_device(): pl.pallas_call(functools.partial(kernel, n), out_shape=jax.ShapeDtypeStru...  116 us
    pallas_call x1, Pallas kernels, on_device(): pl.pallas_call(collect, grid=(groups,), out_shape=jax.ShapeDtypeStruct(pa...  5.48 us

profile of v6, /device:TPU:0, one launch (start us, length us, event | category | flops | bytes accessed | tf_op | source)
XLA Modules:
  0.0 121.5 jit_solution(3221618233261884247)
XLA Ops:
  0.0 116.0 %triangle.1.received = bf16[5,2560,128]{2,1,0:T(8,128)(2,1)} custom-call(bf16[20,640,128]{2,1,0:T(8,128)(2,1)} %pair.1, f32[1,128]{1,0:T(1,128)} %bitcast.6, f32[1,128]{1,0:T(1,128)} %bitcast.7, bf16[128,384]{1,0:T(8,128)(2,1)} %w_qkv.1, bf16[4,128]{1,0:T(4,128)(2,1)} %bitcast.5, bf16[128,128]{1,0:T(8,128)(2,1)} %wgate.1, f32[1,128]{1,0:T(1,128)} %bitcast.8, ...), custom_call_target="tpu_custom_call" | custom-call | tf_op jit(solution)/shard_map/triangle/pallas_call | solution.py:390
  116.0 5.5 %collect.1 = bf16[20,640,128]{2,1,0:T(8,128)(2,1)} custom-call(bf16[5,2560,128]{2,1,0:T(8,128)(2,1)} %triangle.1.received), custom_call_target="tpu_custom_call" | custom-call | tf_op jit(solution)/shard_map/collect/pallas_call | solution.py:425
